TPU v7x, 128 devices: a whole 4x4x4 slice. The times are simulated.
128 devices in a mesh: fsdp: 64 (over z, y_lo, x, core), rep: 2 (over y_hi).
Axes of the slice: x: 4, y: 4 (y_hi: 2, y_lo: 2; y = y_hi * 2 + y_lo), z: 4, core: 2. Of those that a mesh axis runs over, the one named last changes fastest.
Arguments:
- tokens: bfloat16 [16384, 1536], P(('fsdp', 'rep')), may hold values from -6 to 6
- segment_ids: int32 [128, 128], P(('fsdp', 'rep')), may hold values from 0 to 31, never falling along the last dimension, each value on 1 to 64 neighbouring positions
- routes: int32 [16384, 6], P(('fsdp', 'rep')), may hold values from 0 to 63, all different within a row; in each aligned block of 128 rows (0 to 127, 128 to 255, ...) at most 24 rows name the same one
- cotangent: bfloat16 [16384, 1536], P(('fsdp', 'rep')), may hold values from -6 to 6
- query_weight: bfloat16 [1536, 1536], P(('fsdp', 'rep')), may hold values from -0.15625 to 0.15625
- key_weight: bfloat16 [1536, 512], P(('fsdp', 'rep')), may hold values from -0.15625 to 0.15625
- value_weight: bfloat16 [1536, 512], P(('fsdp', 'rep')), may hold values from -0.15625 to 0.15625
- output_weight: bfloat16 [1536, 1536], P(('fsdp', 'rep')), may hold values from -0.625 to 0.625
- shared_gate: bfloat16 [1536, 1024], P(('fsdp', 'rep')), may hold values from -0.15625 to 0.15625
- shared_up: bfloat16 [1536, 1024], P(('fsdp', 'rep')), may hold values from -0.15625 to 0.15625
- shared_down: bfloat16 [1024, 1536], P(('fsdp', 'rep')), may hold values from -0.25 to 0.25
- router_weight: bfloat16 [1536, 64], P(('fsdp', 'rep')), may hold values from -0.078125 to 0.078125
- first_gain: bfloat16 [1536], P(('fsdp', 'rep')), may hold values from 0.099609375 to 1.8984375
- second_gain: bfloat16 [1536], P(('fsdp', 'rep')), may hold values from 0.099609375 to 1.8984375
- expert_gate: bfloat16 [64, 1536, 512], P('fsdp', None, 'rep'), may hold values from -0.15625 to 0.15625
- expert_up: bfloat16 [64, 1536, 512], P('fsdp', None, 'rep'), may hold values from -0.15625 to 0.15625
- expert_down: bfloat16 [64, 512, 1536], P('fsdp', 'rep'), may hold values from -0.75 to 0.75
Outputs:
- block_out: bfloat16 [16384, 1536], P(('fsdp', 'rep'))
- grad_tokens: float32 [16384, 1536], P(('fsdp', 'rep'))
- grad_query_weight: float32 [1536, 1536], P(('fsdp', 'rep'))
- grad_key_weight: float32 [1536, 512], P(('fsdp', 'rep'))
- grad_value_weight: float32 [1536, 512], P(('fsdp', 'rep'))
- grad_output_weight: float32 [1536, 1536], P(('fsdp', 'rep'))
- grad_shared_gate: float32 [1536, 1024], P(('fsdp', 'rep'))
- grad_shared_up: float32 [1536, 1024], P(('fsdp', 'rep'))
- grad_shared_down: float32 [1024, 1536], P(('fsdp', 'rep'))
- grad_router_weight: float32 [1536, 64], P(('fsdp', 'rep'))
- grad_first_gain: float32 [1536], P(('fsdp', 'rep'))
- grad_second_gain: float32 [1536], P(('fsdp', 'rep'))
- grad_expert_gate: float32 [64, 1536, 512], P('fsdp', None, 'rep')
- grad_expert_up: float32 [64, 1536, 512], P('fsdp', None, 'rep')
- grad_expert_down: float32 [64, 512, 1536], P('fsdp', 'rep')
Inputs may be any that keep to these rules, and one draw needn't show every extreme that they name: `routes`: among the 128 rows of one device no expert is named by more than 24 rows, a bound that some block reaches; a row names 6 different experts. `segment_ids`: within a device's row the numbers never fall; a sequence holds 1 to 64 tokens, one exactly 64.
All inputs are finite; a program needn't handle non-finite values.
Results may differ from a plain program's by a relative error of at most 0.024.
Values may be sent and summed in bfloat16 or wider, within the bound.
A program may use at most 256 MiB of HBM per device.

v0:
```python
import math

import jax
import jax.numpy as jnp
from jax import lax
from jax.sharding import PartitionSpec as P

D = 1536
HEADS = 12
KV_HEADS = 4
HEAD_DIM = 128
TOP = 6
KVD = 512


epsilon = 1e-06


def rms_scale(values):
    return lax.rsqrt(jnp.mean(values * values, axis=-1, keepdims=True) + epsilon)


def silu_parts(pre):
    sigma = jax.nn.sigmoid(pre)
    return (pre * sigma, sigma * (1.0 + pre * (1.0 - sigma)))


def norm_back(grad_normed, source, scale, gain):
    weighted = grad_normed * gain
    inner = jnp.mean(weighted * source, axis=-1, keepdims=True)
    grad_source = scale * weighted - source * (scale * scale * scale) * inner
    grad_gain = jnp.sum(grad_normed * source * scale, axis=0)
    return (grad_source, grad_gain)


def matmul(left, right):
    return jnp.dot(left, right, preferred_element_type=jnp.float32)


def right_transposed(left, right):
    return lax.dot_general(
        left, right, (((1,), (1,)), ((), ())), preferred_element_type=jnp.float32
    )


def left_transposed(left, right):
    return lax.dot_general(
        left, right, (((0,), (0,)), ((), ())), preferred_element_type=jnp.float32
    )


def local(
    tokens,
    segment_ids,
    routes,
    cotangent,
    query_weight,
    key_weight,
    value_weight,
    output_weight,
    shared_gate,
    shared_up,
    shared_down,
    router_weight,
    first_gain,
    second_gain,
    expert_gate,
    expert_up,
    expert_down,
):
    gathered = (
        lax.all_gather(query_weight, ("fsdp", "rep"), axis=0, tiled=True),
        lax.all_gather(key_weight, ("fsdp", "rep"), axis=0, tiled=True),
        lax.all_gather(value_weight, ("fsdp", "rep"), axis=0, tiled=True),
        lax.all_gather(output_weight, ("fsdp", "rep"), axis=0, tiled=True),
        lax.all_gather(shared_gate, ("fsdp", "rep"), axis=0, tiled=True),
        lax.all_gather(shared_up, ("fsdp", "rep"), axis=0, tiled=True),
        lax.all_gather(shared_down, ("fsdp", "rep"), axis=0, tiled=True),
        lax.all_gather(router_weight, ("fsdp", "rep"), axis=0, tiled=True),
        lax.all_gather(first_gain, ("fsdp", "rep"), axis=0, tiled=True),
        lax.all_gather(second_gain, ("fsdp", "rep"), axis=0, tiled=True),
    )
    (
        w_query,
        w_key,
        w_value,
        w_output,
        w_sgate,
        w_sup,
        w_sdown,
        w_router,
        gain_low_one,
        gain_low_two,
    ) = gathered
    gain_one = gain_low_one.astype(jnp.float32)
    gain_two = gain_low_two.astype(jnp.float32)
    gate_whole, up_whole, down_whole = (
        lax.all_gather(expert_gate, "rep", axis=2, tiled=True),
        lax.all_gather(expert_up, "rep", axis=2, tiled=True),
        lax.all_gather(expert_down, "rep", axis=1, tiled=True),
    )
    gate_full = gate_whole[0]
    up_full = up_whole[0]
    down_full = down_whole[0]
    rows = tokens.shape[0]
    groups = HEADS // KV_HEADS
    scale = 1.0 / math.sqrt(HEAD_DIM)
    source = tokens.astype(jnp.float32)
    scale_one = rms_scale(source)
    normed = (source * scale_one * gain_one).astype(jnp.bfloat16)
    query = matmul(normed, w_query).astype(jnp.bfloat16)
    keys = matmul(normed, w_key).astype(jnp.bfloat16)
    values = matmul(normed, w_value).astype(jnp.bfloat16)
    query_heads = query.reshape(rows, KV_HEADS, groups, HEAD_DIM)
    key_heads = keys.reshape(rows, KV_HEADS, HEAD_DIM)
    value_heads = values.reshape(rows, KV_HEADS, HEAD_DIM)
    segment = segment_ids[0]
    position = jnp.arange(rows)
    allowed = (segment[:, None] == segment[None, :]) & (position[:, None] >= position[None, :])

    def masked_scores():
        raw = (
            jnp.einsum("tkgd,skd->kgts", query_heads, key_heads, preferred_element_type=jnp.float32)
            * scale
        )
        return jnp.where(allowed, raw, -1e30)

    scores = masked_scores()
    peak = jnp.max(scores, axis=-1, keepdims=True)
    expo = jnp.exp(scores - peak)
    total = jnp.sum(expo, axis=-1, keepdims=True)
    log_total = peak + jnp.log(total)
    probs_low = (expo / total).astype(jnp.bfloat16)
    attended = (
        jnp.einsum("kgts,skd->tkgd", probs_low, value_heads, preferred_element_type=jnp.float32)
        .reshape(rows, D)
        .astype(jnp.bfloat16)
    )
    resid = source + matmul(attended, w_output)
    scale_two = rms_scale(resid)
    normed_two = (resid * scale_two * gain_two).astype(jnp.bfloat16)
    logits = matmul(normed_two, w_router)
    gates = jax.nn.softmax(jnp.take_along_axis(logits, routes, axis=1), axis=-1)
    shared_pre_gate = matmul(normed_two, w_sgate)
    shared_pre_up = matmul(normed_two, w_sup)
    shared_act, shared_slope = silu_parts(shared_pre_gate)
    shared_hidden = (shared_act * shared_pre_up).astype(jnp.bfloat16)
    shared_out = matmul(shared_hidden, w_sdown)
    experts_total = expert_gate.shape[0] * lax.axis_size("fsdp")
    capacity = 2 * rows * TOP // experts_total
    flat_expert = routes.reshape(-1)
    assigned = flat_expert.shape[0]
    onehot = (flat_expert[:, None] == jnp.arange(experts_total, dtype=jnp.int32)[None, :]).astype(
        jnp.int32
    )
    place = jnp.sum((jnp.cumsum(onehot, axis=0) - onehot) * onehot, axis=1)
    slots = flat_expert * capacity + place
    owner = jnp.arange(assigned, dtype=jnp.int32) // TOP
    outgoing = (
        jnp.zeros((experts_total * capacity, D), jnp.bfloat16).at[slots].set(normed_two[owner])
    )
    outgoing = outgoing.reshape(experts_total, capacity, D)
    arrived = lax.all_to_all(outgoing, "fsdp", split_axis=0, concat_axis=0, tiled=True)
    pre_gate = jnp.einsum("skd,dh->skh", arrived, gate_full, preferred_element_type=jnp.float32)
    pre_up = jnp.einsum("skd,dh->skh", arrived, up_full, preferred_element_type=jnp.float32)
    activated, unused = silu_parts(pre_gate)
    hidden = (activated * pre_up).astype(jnp.bfloat16)
    produced = jnp.einsum(
        "skh,hd->skd", hidden, down_full, preferred_element_type=jnp.float32
    ).astype(jnp.bfloat16)
    returned = lax.all_to_all(produced, "fsdp", split_axis=0, concat_axis=0, tiled=True)
    returned, arrived, pre_gate, pre_up = (returned, arrived, pre_gate, pre_up)
    slot_out = (
        returned.reshape(experts_total * capacity, D)[slots]
        .astype(jnp.float32)
        .reshape(rows, TOP, D)
    )
    final = resid + shared_out + jnp.sum(gates[:, :, None] * slot_out, axis=1)
    block_out = final.astype(jnp.bfloat16)
    regathered = (
        lax.all_gather(query_weight, ("fsdp", "rep"), axis=0, tiled=True),
        lax.all_gather(key_weight, ("fsdp", "rep"), axis=0, tiled=True),
        lax.all_gather(value_weight, ("fsdp", "rep"), axis=0, tiled=True),
        lax.all_gather(output_weight, ("fsdp", "rep"), axis=0, tiled=True),
        lax.all_gather(shared_gate, ("fsdp", "rep"), axis=0, tiled=True),
        lax.all_gather(shared_up, ("fsdp", "rep"), axis=0, tiled=True),
        lax.all_gather(shared_down, ("fsdp", "rep"), axis=0, tiled=True),
        lax.all_gather(router_weight, ("fsdp", "rep"), axis=0, tiled=True),
        lax.all_gather(first_gain, ("fsdp", "rep"), axis=0, tiled=True),
        lax.all_gather(second_gain, ("fsdp", "rep"), axis=0, tiled=True),
    )
    (
        w_query,
        w_key,
        w_value,
        w_output,
        w_sgate,
        w_sup,
        w_sdown,
        w_router,
        gain_low_one,
        gain_low_two,
    ) = regathered
    gain_one = gain_low_one.astype(jnp.float32)
    gain_two = gain_low_two.astype(jnp.float32)
    grad_final = cotangent.astype(jnp.float32)
    grad_gates = jnp.sum(slot_out * grad_final[:, None, :], axis=-1)
    slot_grad = (
        (gates[:, :, None] * grad_final[:, None, :]).astype(jnp.bfloat16).reshape(assigned, D)
    )
    grad_outgoing = jnp.zeros((experts_total * capacity, D), jnp.bfloat16).at[slots].set(slot_grad)
    grad_outgoing = grad_outgoing.reshape(experts_total, capacity, D)
    grad_arrived = lax.all_to_all(grad_outgoing, "fsdp", split_axis=0, concat_axis=0, tiled=True)
    grad_hidden = jnp.einsum(
        "skd,hd->skh", grad_arrived, down_full, preferred_element_type=jnp.float32
    )
    activated, slope = silu_parts(pre_gate)
    hidden = (activated * pre_up).astype(jnp.bfloat16)
    grad_down_local = jnp.einsum(
        "skh,skd->hd", hidden, grad_arrived, preferred_element_type=jnp.float32
    )
    grad_gate_pre = (grad_hidden * pre_up * slope).astype(jnp.bfloat16)
    grad_up_pre = (grad_hidden * activated).astype(jnp.bfloat16)
    grad_gate_local = jnp.einsum(
        "skd,skh->dh", arrived, grad_gate_pre, preferred_element_type=jnp.float32
    )
    grad_up_local = jnp.einsum(
        "skd,skh->dh", arrived, grad_up_pre, preferred_element_type=jnp.float32
    )
    slot_back = jnp.einsum(
        "skh,dh->skd", grad_gate_pre, gate_full, preferred_element_type=jnp.float32
    ) + jnp.einsum("skh,dh->skd", grad_up_pre, up_full, preferred_element_type=jnp.float32)
    grad_returned = lax.all_to_all(
        slot_back.astype(jnp.bfloat16), "fsdp", split_axis=0, concat_axis=0, tiled=True
    )
    grad_normed_two = jnp.sum(
        grad_returned.reshape(experts_total * capacity, D)[slots]
        .astype(jnp.float32)
        .reshape(rows, TOP, D),
        axis=1,
    )
    mean_gate = jnp.sum(gates * grad_gates, axis=1, keepdims=True)
    grad_chosen = gates * (grad_gates - mean_gate)
    route_hits = (
        routes[:, :, None] == jnp.arange(experts_total, dtype=jnp.int32)[None, None, :]
    ).astype(jnp.float32)
    grad_logits = jnp.sum(route_hits * grad_chosen[:, :, None], axis=1).astype(jnp.bfloat16)
    grad_router = left_transposed(normed_two, grad_logits)
    grad_normed_two = grad_normed_two + right_transposed(grad_logits, w_router)
    grad_shared_out = grad_final.astype(jnp.bfloat16)
    grad_sdown = left_transposed(shared_hidden, grad_shared_out)
    grad_shared_hidden = right_transposed(grad_shared_out, w_sdown)
    grad_shared_gate_pre = (grad_shared_hidden * shared_pre_up * shared_slope).astype(jnp.bfloat16)
    grad_shared_up_pre = (grad_shared_hidden * shared_act).astype(jnp.bfloat16)
    grad_sgate = left_transposed(normed_two, grad_shared_gate_pre)
    grad_sup = left_transposed(normed_two, grad_shared_up_pre)
    grad_normed_two = (
        grad_normed_two
        + right_transposed(grad_shared_gate_pre, w_sgate)
        + right_transposed(grad_shared_up_pre, w_sup)
    )
    grad_resid_norm, grad_gain_two = norm_back(grad_normed_two, resid, scale_two, gain_two)
    grad_resid = grad_final + grad_resid_norm
    grad_out_one = grad_resid.astype(jnp.bfloat16)
    grad_woutput = left_transposed(attended, grad_out_one)
    grad_attended = right_transposed(grad_out_one, w_output).astype(jnp.bfloat16)
    grad_attended = grad_attended.reshape(rows, KV_HEADS, groups, HEAD_DIM)
    probs = jnp.exp(masked_scores() - log_total)
    probs_again = probs.astype(jnp.bfloat16)
    grad_probs = jnp.einsum(
        "tkgd,skd->kgts", grad_attended, value_heads, preferred_element_type=jnp.float32
    )
    grad_values = (
        jnp.einsum("kgts,tkgd->skd", probs_again, grad_attended, preferred_element_type=jnp.float32)
        .reshape(rows, KVD)
        .astype(jnp.bfloat16)
    )
    grad_scores = (
        probs * (grad_probs - jnp.sum(probs * grad_probs, axis=-1, keepdims=True))
    ).astype(jnp.bfloat16)
    grad_query = (
        (
            jnp.einsum("kgts,skd->tkgd", grad_scores, key_heads, preferred_element_type=jnp.float32)
            * scale
        )
        .reshape(rows, D)
        .astype(jnp.bfloat16)
    )
    grad_keys = (
        (
            jnp.einsum(
                "kgts,tkgd->skd", grad_scores, query_heads, preferred_element_type=jnp.float32
            )
            * scale
        )
        .reshape(rows, KVD)
        .astype(jnp.bfloat16)
    )
    grad_wquery = left_transposed(normed, grad_query)
    grad_wkey = left_transposed(normed, grad_keys)
    grad_wvalue = left_transposed(normed, grad_values)
    grad_normed = (
        right_transposed(grad_query, w_query)
        + right_transposed(grad_keys, w_key)
        + right_transposed(grad_values, w_value)
    )
    grad_source_norm, grad_gain_one = norm_back(grad_normed, source, scale_one, gain_one)
    grad_tokens = grad_resid + grad_source_norm
    summed = (
        lax.psum_scatter(grad_wquery, ("fsdp", "rep"), scatter_dimension=0, tiled=True),
        lax.psum_scatter(grad_wkey, ("fsdp", "rep"), scatter_dimension=0, tiled=True),
        lax.psum_scatter(grad_wvalue, ("fsdp", "rep"), scatter_dimension=0, tiled=True),
        lax.psum_scatter(grad_woutput, ("fsdp", "rep"), scatter_dimension=0, tiled=True),
        lax.psum_scatter(grad_sgate, ("fsdp", "rep"), scatter_dimension=0, tiled=True),
        lax.psum_scatter(grad_sup, ("fsdp", "rep"), scatter_dimension=0, tiled=True),
        lax.psum_scatter(grad_sdown, ("fsdp", "rep"), scatter_dimension=0, tiled=True),
        lax.psum_scatter(grad_router, ("fsdp", "rep"), scatter_dimension=0, tiled=True),
        lax.psum_scatter(grad_gain_one, ("fsdp", "rep"), scatter_dimension=0, tiled=True),
        lax.psum_scatter(grad_gain_two, ("fsdp", "rep"), scatter_dimension=0, tiled=True),
    )
    expert_summed = (
        lax.psum_scatter(
            grad_gate_local[None].astype(jnp.bfloat16), "rep", scatter_dimension=2, tiled=True
        ).astype(jnp.float32),
        lax.psum_scatter(
            grad_up_local[None].astype(jnp.bfloat16), "rep", scatter_dimension=2, tiled=True
        ).astype(jnp.float32),
        lax.psum_scatter(
            grad_down_local[None].astype(jnp.bfloat16), "rep", scatter_dimension=1, tiled=True
        ).astype(jnp.float32),
    )
    return (
        block_out,
        grad_tokens,
        summed[0],
        summed[1],
        summed[2],
        summed[3],
        summed[4],
        summed[5],
        summed[6],
        summed[7],
        summed[8],
        summed[9],
        expert_summed[0],
        expert_summed[1],
        expert_summed[2],
    )


def solution(mesh):
    in_specs = (
        P(("fsdp", "rep"), None),
        P(("fsdp", "rep"), None),
        P(("fsdp", "rep"), None),
        P(("fsdp", "rep"), None),
        P(("fsdp", "rep"), None),
        P(("fsdp", "rep"), None),
        P(("fsdp", "rep"), None),
        P(("fsdp", "rep"), None),
        P(("fsdp", "rep"), None),
        P(("fsdp", "rep"), None),
        P(("fsdp", "rep"), None),
        P(("fsdp", "rep"), None),
        P(("fsdp", "rep")),
        P(("fsdp", "rep")),
        P("fsdp", None, "rep"),
        P("fsdp", None, "rep"),
        P("fsdp", "rep", None),
    )
    out_specs = (
        P(("fsdp", "rep"), None),
        P(("fsdp", "rep"), None),
        P(("fsdp", "rep"), None),
        P(("fsdp", "rep"), None),
        P(("fsdp", "rep"), None),
        P(("fsdp", "rep"), None),
        P(("fsdp", "rep"), None),
        P(("fsdp", "rep"), None),
        P(("fsdp", "rep"), None),
        P(("fsdp", "rep"), None),
        P(("fsdp", "rep")),
        P(("fsdp", "rep")),
        P("fsdp", None, "rep"),
        P("fsdp", None, "rep"),
        P("fsdp", "rep", None),
    )
    return jax.shard_map(local, mesh=mesh, in_specs=in_specs, out_specs=out_specs, check_vma=False)
```

profile of v0, /device:TPU:1, one launch (start us, length us, event | category | flops | bytes accessed | tf_op | source)
XLA Modules:
  0.0 4647.3 jit_solution(10532386676052684565)
XLA Ops:
  17.4 68.9 %all-reduce.19 = (bf16[1536]{0:T(1024)(128)(2,1)S(1)}, bf16[1536]{0:T(1024)(128)(2,1)S(1)}) all-reduce(bf16[1536]{0:T(1024)(128)(2,1)S(1)} %dynamic-update-slice, bf16[1536]{0:T(1024)(128)(2,1)S(1)} %dynamic-update-slice.1), channel_id=1, replica_groups=mesh['fsdp'=64,'rep'=2] {'fsdp','rep'}, use_global_device_ids=true, to_apply=%add | all-reduce | flops 3072 | bytes 12288
  87.3 225.4 %all-gather.28.cloned.1.call-done = bf16[128,12,512]{2,1,0:T(8,128)(2,1)} async-done(((bf16[1,12,512]{2,1,0:T(8,128)(2,1)}), bf16[128,12,512]{2,1,0:T(8,128)(2,1)}) %all-gather.28.cloned.1.call-update) | async-done | bytes 1572880 | tf_op jit(solution)/shard_map/all_gather | solution.py:73
  316.3 299.5 %all-gather.26.cloned.1.call-done = bf16[128,12,512]{2,1,0:T(8,128)(2,1)} async-done(((bf16[1,12,512]{2,1,0:T(8,128)(2,1)}), bf16[128,12,512]{2,1,0:T(8,128)(2,1)}) %all-gather.26.cloned.1.call-update) | async-done | bytes 1572880 | tf_op jit(solution)/shard_map/all_gather | solution.py:74
  618.8 310.9 %all-gather.30.cloned.1.call-done = bf16[128,12,1536]{2,1,0:T(8,128)(2,1)} async-done(((bf16[1,12,1536]{2,1,0:T(8,128)(2,1)}), bf16[128,12,1536]{2,1,0:T(8,128)(2,1)}) %all-gather.30.cloned.1.call-update) | async-done | bytes 4718608 | tf_op jit(solution)/shard_map/all_gather | solution.py:72
  929.7 8.2 reshape.355
  941.3 301.9 %all-gather.32.cloned.1.call-done = bf16[128,12,1536]{2,1,0:T(8,128)(2,1)} async-done(((bf16[1,12,1536]{2,1,0:T(8,128)(2,1)}), bf16[128,12,1536]{2,1,0:T(8,128)(2,1)}) %all-gather.32.cloned.1.call-update) | async-done | bytes 4718608 | tf_op jit(solution)/shard_map/all_gather | solution.py:75
  1243.2 8.2 reshape.357
  1255.9 19.6 scatter_custom_fusion
  1275.5 8.1 all-to-all-start
  1287.8 6.6 mul.317
  1294.5 364.2 %all-gather.6 = bf16[128,12,64]{2,1,0:T(8,128)(2,1)S(1)} all-gather(bf16[1,12,64]{2,1,0:T(8,128)(2,1)S(1)} %bitcast.202), channel_id=1, replica_groups=mesh['fsdp'=64,'rep'=2] {'fsdp','rep'}, dimensions={0}, use_global_device_ids=true | all-gather | bytes 198144 | tf_op jit(solution)/shard_map/all_gather | solution.py:79
  1665.1 14.2 scatter_custom_fusion.1
  1679.4 8.8 all-to-all-start.2
  1688.7 7.2 fusion.30
  1695.9 7.1 fusion.26
  1703.0 43.1 all-to-all-done.2
  1746.1 10.3 multiply_convert_fusion.1
  1761.9 8.7 all-to-all-start.1
  1770.6 6.1 fusion.13
  1777.0 6.8 fusion.12
  1792.5 35.9 all-to-all-done.1
  1828.4 9.3 all-to-all-start.3
  1837.7 6.1 fusion.11
  1845.7 6.2 reshape.359
  1851.8 247.9 %all-gather.36.cloned.1.call-done = bf16[128,12,1024]{2,1,0:T(8,128)(2,1)} async-done(((bf16[1,12,1024]{2,1,0:T(8,128)(2,1)}), bf16[128,12,1024]{2,1,0:T(8,128)(2,1)}) %all-gather.36.cloned.1.call-update) | async-done | bytes 3145744 | tf_op jit(solution)/shard_map/all_gather | solution.py:77
  2109.1 306.4 %all-gather.18.cloned.1.call-done = bf16[1024,1536]{1,0:T(8,128)(2,1)} async-done(((bf16[8,1536]{1,0:T(8,128)(2,1)}), bf16[1024,1536]{1,0:T(8,128)(2,1)}) %all-gather.18.cloned.1.call-update) | async-done | bytes 3145744 | tf_op jit(solution)/shard_map/all_gather | solution.py:78
  2434.5 8.9 gather_fusion
  2448.4 8.9 gather_fusion.1
  2462.4 6.1 multiply_reduce_fusion
  2470.0 5.6 reduce_sum.144
  2501.6 1240.5 %fusion.79 = (f32[16,1536]{1,0:T(8,128)S(1)}, f32[16,512]{1,0:T(8,128)S(1)}, f32[16,512]{1,0:T(8,128)S(1)}, f32[16,1536]{1,0:T(8,128)S(1)}, f32[16,1024]{1,0:T(8...) fusion(f32[1536,1536]{1,0:T(8,128)} %fusion.74, f32[1536,512]{1,0:T(8,128)} %fusion.72, ...), kind=kCustom, calls=%all-reduce-scatter.7 | all-reduce-scatter fusion | flops 12713985 | bytes 38539264
  3744.7 6.6 collective-permute-start.221
  3762.6 5.9 collective-permute-start.218
  3823.6 5.6 collective-permute-start.198
  3899.7 5.8 collective-permute-start.38
  3909.5 5.5 collective-permute-start.35
  4056.8 5.5 collective-permute-start.134
  4227.4 6.2 collective-permute-start.8
  4269.1 63.3 %all-reduce.18 = (f32[1536]{0:T(1024)S(1)}, f32[1536]{0:T(1024)S(1)}) all-reduce(f32[1536]{0:T(1024)S(1)} %get-tuple-element.19, f32[1536]{0:T(1024)S(1)} %copy-done.205), channel_id=10, replica_groups=mesh['fsdp'=64,'rep'=2] {'fsdp','rep'}, use_global_device_ids=true, to_apply=%region_28.29.clone | all-reduce | flops 3072 | bytes 24576
  4333.6 21.9 concatenate.9
  4372.5 5.4 collective-permute-start.116
  4378.8 7.4 concatenate.4
  4386.2 26.7 concatenate.5
  4438.9 50.5 %concatenate.7 = f32[524,1024]{1,0:T(8,128)} concatenate(f32[12,1024]{1,0:T(8,128)} %copy-done.100, f32[16,1024]{1,0:T(8,128)} %copy-done.99, f32[16,1024]{1,0:T(8,128)} %copy-done.101, f32[16,1024]{1,0:T(8,128)} %copy-done.102, f32[16,1024]{1,0:T(8,128)} %copy-done.103, f32[16,1024]{1,0:T(8,128)} %copy-done.104, f32[16,1024]{1,0:T(8,128)} %copy-done.105, ...), dimensions={0} | concatenate | bytes 4292608
  4489.3 28.6 concatenate.8
  4525.4 5.9 collective-permute-start.102
  4552.9 31.7 concatenate.3
  4584.7 53.4 %concatenate.6 = f32[524,1536]{1,0:T(8,128)} concatenate(f32[12,1536]{1,0:T(8,128)} %copy-done.43, f32[16,1536]{1,0:T(8,128)} %copy-done.74, f32[16,1536]{1,0:T(8,128)} %copy-done.77, f32[16,1536]{1,0:T(8,128)} %copy-done.78, f32[16,1536]{1,0:T(8,128)} %copy-done.79, f32[16,1536]{1,0:T(8,128)} %copy-done.80, f32[16,1536]{1,0:T(8,128)} %copy-done.81, f32[16,1536]{1,0:T(8,128)} %copy-done.82, ...), dimensions={0} | concatenate | bytes 6438912
  (1059 shorter events, 675.9 us)
Async XLA Ops:
  7.2 305.5 %all-gather.28.cloned.1.call-start = ((), (), s32[]{:S(2)}) async-start(), calls=%async_computation.17 | async-start | bytes 2113536 | tf_op jit(solution)/shard_map/all_gather | solution.py:73
  8.0 607.9 %all-gather.26.cloned.1.call-start = ((), (), s32[]{:S(2)}) async-start(), calls=%async_computation.16 | async-start | bytes 2113536 | tf_op jit(solution)/shard_map/all_gather | solution.py:74
  8.7 921.0 %all-gather.30.cloned.1.call-start = ((), (), s32[]{:S(2)}) async-start(), calls=%async_computation.18 | async-start | bytes 6340608 | tf_op jit(solution)/shard_map/all_gather | solution.py:72
  9.4 1233.8 %all-gather.32.cloned.1.call-start = ((), (), s32[]{:S(2)}) async-start(), calls=%async_computation.19 | async-start | bytes 6340608 | tf_op jit(solution)/shard_map/all_gather | solution.py:75
  10.0 1678.7 %all-gather.20.cloned.1.call-start = ((), (), s32[]{:S(2)}) async-start(), calls=%async_computation.9 | async-start | bytes 2359296 | tf_op jit(solution)/shard_map/all_gather | solution.py:98
  10.6 1685.3 %all-gather.22.cloned.1.call-start = ((), (), s32[]{:S(2)}) async-start(), calls=%async_computation.10 | async-start | bytes 2359296 | tf_op jit(solution)/shard_map/all_gather | solution.py:99
  11.2 1691.9 %all-gather.24.cloned.1.call-start = ((), (), s32[]{:S(2)}) async-start(), calls=%async_computation.11 | async-start | bytes 2359296 | tf_op jit(solution)/shard_map/all_gather | solution.py:100
  11.9 1833.7 %all-gather.34.cloned.1.call-start = ((), (), s32[]{:S(2)}) async-start(), calls=%async_computation.20 | async-start | bytes 4227072 | tf_op jit(solution)/shard_map/all_gather | solution.py:76
  1275.5 403.8 %all-to-all-start = ((bf16[64,24,1536]{2,1,0:T(8,128)(2,1)}), bf16[64,24,1536]{2,1,0:T(8,128)(2,1)}, u32[]{:S(2)}, u32[]{:S(2)}) async-start(bf16[64,24,1536]{2,1,0:T(8,128)(2,1)} %bitcast.178), calls=%async_computation | async-start | bytes 9437184 | tf_op jit(solution)/shard_map/all_to_all | solution.py:163
  1283.6 816.1 %all-gather.36.cloned.1.call-start = ((), (), s32[]{:S(2)}) async-start(), calls=%async_computation.21 | async-start | bytes 4227072 | tf_op jit(solution)/shard_map/all_gather | solution.py:77
  1679.4 66.8 %all-to-all-start.2 = ((bf16[64,24,1536]{2,1,0:T(8,128)(2,1)}), bf16[64,24,1536]{2,1,0:T(8,128)(2,1)}, u32[]{:S(2)}, u32[]{:S(2)}) async-start(bf16[64,24,1536]{2,1,0:T(8,128)(2,1)} %bitcast.179), calls=%async_computation.2 | async-start | bytes 9437184 | tf_op jit(solution)/shard_map/all_to_all | solution.py:213
  1688.1 727.3 %all-gather.18.cloned.1.call-start = ((), (), s32[]{:S(2)}) async-start(), calls=%async_computation.8 | async-start | bytes 3170304 | tf_op jit(solution)/shard_map/all_gather | solution.py:78
  1761.9 66.5 %all-to-all-start.1 = ((bf16[64,24,1536]{2,1,0:T(8,128)(2,1)}), bf16[64,24,1536]{2,1,0:T(8,128)(2,1)}, u32[]{:S(2)}, u32[]{:S(2)}) async-start(bf16[64,24,1536]{2,1,0:T(8,128)(2,1)} %convolution_convert_fusion), calls=%async_computation.1 | async-start | bytes 9437184 | tf_op jit(solution)/shard_map/all_to_all | solution.py:171
  1770.5 2407.4 %reduce-scatter.21.cloned.1.call-start = ((), (), s32[]{:S(2)}) async-start(), calls=%async_computation.13 | async-start | bytes 2359296 | tf_op jit(solution)/shard_map/reduce_scatter | solution.py:322
  1776.7 2403.6 %reduce-scatter.23.cloned.1.call-start = ((), (), s32[]{:S(2)}) async-start(), calls=%async_computation.14 | async-start | bytes 2359296 | tf_op jit(solution)/shard_map/reduce_scatter | solution.py:325
  1828.4 620.0 %all-to-all-start.3 = ((bf16[64,24,1536]{2,1,0:T(8,128)(2,1)}), bf16[64,24,1536]{2,1,0:T(8,128)(2,1)}, u32[]{:S(2)}, u32[]{:S(2)}) async-start(bf16[64,24,1536]{2,1,0:T(8,128)(2,1)} %add_convert_fusion), calls=%async_computation.3 | async-start | bytes 9437184 | tf_op jit(solution)/shard_map/all_to_all | solution.py:233
  1837.7 2345.1 %reduce-scatter.25.cloned.1.call-start = ((), (), s32[]{:S(2)}) async-start(), calls=%async_computation.15 | async-start | bytes 2359296 | tf_op jit(solution)/shard_map/reduce_scatter | solution.py:328
  1843.8 2796.5 %reduce-scatter.19.cloned.1.call-start = ((), (), s32[]{:S(2)}) async-start(), calls=%async_computation.12 | async-start | bytes 6340608 | tf_op jit(solution)/shard_map/reduce_scatter | solution.py:316
  3742.1 26.4 collective-permute-start.222
  3744.7 27.9 collective-permute-start.221
  3751.4 26.6 collective-permute-start.220
  3754.8 25.2 collective-permute-start.219
  3762.6 20.0 collective-permute-start.218
  3811.7 40.7 collective-permute-start.63
  3813.0 40.7 collective-permute-start.95
  4154.5 20.2 collective-permute-start.30
  4156.6 19.6 collective-permute-start.29
  4259.9 95.6 %collective-permute-start.125 = (f32[16,1536]{1,0:T(8,128)S(1)}, f32[16,1536]{1,0:T(8,128)S(1)}, u32[]{:S(2)}, u32[]{:S(2)}) collective-permute-start(f32[16,1536]{1,0:T(8,128)S(1)} %get-tuple-element.35), channel_id=1, source_target_pairs={{0,30},{1,31},{2,32},{3,33},{4,34},{5,35},{6,36},{7,37},{8,38},{9,... | collective-permute-start | bytes 294920
  4261.3 98.3 %collective-permute-start.124 = (f32[16,1536]{1,0:T(8,128)S(1)}, f32[16,1536]{1,0:T(8,128)S(1)}, u32[]{:S(2)}, u32[]{:S(2)}) collective-permute-start(f32[16,1536]{1,0:T(8,128)S(1)} %get-tuple-element.35), channel_id=1, source_target_pairs={{0,29},{1,30},{2,31},{3,32},{4,33},{5,34},{6,35},{7,36},{8,37},{9,... | collective-permute-start | bytes 294920
  4262.8 100.7 %collective-permute-start.123 = (f32[16,1536]{1,0:T(8,128)S(1)}, f32[16,1536]{1,0:T(8,128)S(1)}, u32[]{:S(2)}, u32[]{:S(2)}) collective-permute-start(f32[16,1536]{1,0:T(8,128)S(1)} %get-tuple-element.35), channel_id=1, source_target_pairs={{0,28},{1,29},{2,30},{3,31},{4,32},{5,33},{6,34},{7,35},{8,36},{9,... | collective-permute-start | bytes 294920
  4264.7 104.1 %collective-permute-start.122 = (f32[16,1536]{1,0:T(8,128)S(1)}, f32[16,1536]{1,0:T(8,128)S(1)}, u32[]{:S(2)}, u32[]{:S(2)}) collective-permute-start(f32[16,1536]{1,0:T(8,128)S(1)} %get-tuple-element.35), channel_id=1, source_target_pairs={{0,27},{1,28},{2,29},{3,30},{4,31},{5,32},{6,33},{7,34},{8,35},{9,... | collective-permute-start | bytes 294920
  4266.3 106.2 %collective-permute-start.121 = (f32[16,1536]{1,0:T(8,128)S(1)}, f32[16,1536]{1,0:T(8,128)S(1)}, u32[]{:S(2)}, u32[]{:S(2)}) collective-permute-start(f32[16,1536]{1,0:T(8,128)S(1)} %get-tuple-element.35), channel_id=1, source_target_pairs={{0,26},{1,27},{2,28},{3,29},{4,30},{5,31},{6,32},{7,33},{8,34},{9,... | collective-permute-start | bytes 294920
  4355.5 57.3 %collective-permute-start.120 = (f32[16,1536]{1,0:T(8,128)S(1)}, f32[16,1536]{1,0:T(8,128)S(1)}, u32[]{:S(2)}, u32[]{:S(2)}) collective-permute-start(f32[16,1536]{1,0:T(8,128)S(1)} %get-tuple-element.35), channel_id=1, source_target_pairs={{0,25},{1,26},{2,27},{3,28},{4,29},{5,30},{6,31},{7,32},{8,33},{9,... | collective-permute-start | bytes 294920
  4359.7 54.5 %collective-permute-start.119 = (f32[16,1536]{1,0:T(8,128)S(1)}, f32[16,1536]{1,0:T(8,128)S(1)}, u32[]{:S(2)}, u32[]{:S(2)}) collective-permute-start(f32[16,1536]{1,0:T(8,128)S(1)} %get-tuple-element.35), channel_id=1, source_target_pairs={{0,24},{1,25},{2,26},{3,27},{4,28},{5,29},{6,30},{7,31},{8,32},{9,... | collective-permute-start | bytes 294920
  4363.5 53.3 %collective-permute-start.118 = (f32[16,1536]{1,0:T(8,128)S(1)}, f32[16,1536]{1,0:T(8,128)S(1)}, u32[]{:S(2)}, u32[]{:S(2)}) collective-permute-start(f32[16,1536]{1,0:T(8,128)S(1)} %get-tuple-element.35), channel_id=1, source_target_pairs={{0,23},{1,24},{2,25},{3,26},{4,27},{5,28},{6,29},{7,30},{8,31},{9,... | collective-permute-start | bytes 294920
  4368.8 49.6 %collective-permute-start.117 = (f32[16,1536]{1,0:T(8,128)S(1)}, f32[16,1536]{1,0:T(8,128)}, u32[]{:S(2)}, u32[]{:S(2)}) collective-permute-start(f32[16,1536]{1,0:T(8,128)S(1)} %get-tuple-element.35), channel_id=1, source_target_pairs={{0,22},{1,23},{2,24},{3,25},{4,26},{5,27},{6,28},{7,29},{8,30},{9,... | collective-permute-start | bytes 294920
  4372.5 48.1 %collective-permute-start.116 = (f32[16,1536]{1,0:T(8,128)S(1)}, f32[16,1536]{1,0:T(8,128)}, u32[]{:S(2)}, u32[]{:S(2)}) collective-permute-start(f32[16,1536]{1,0:T(8,128)S(1)} %get-tuple-element.35), channel_id=1, source_target_pairs={{0,21},{1,22},{2,23},{3,24},{4,25},{5,26},{6,27},{7,28},{8,29},{9,... | collective-permute-start | bytes 294920
  4422.5 95.5 %collective-permute-start.110 = (f32[16,1536]{1,0:T(8,128)S(1)}, f32[16,1536]{1,0:T(8,128)}, u32[]{:S(2)}, u32[]{:S(2)}) collective-permute-start(f32[16,1536]{1,0:T(8,128)S(1)} %get-tuple-element.35), channel_id=1, source_target_pairs={{0,15},{1,16},{2,17},{3,18},{4,19},{5,20},{6,21},{7,22},{8,23},{9,... | collective-permute-start | bytes 294920
  4425.7 93.6 %collective-permute-start.109 = (f32[16,1536]{1,0:T(8,128)S(1)}, f32[16,1536]{1,0:T(8,128)}, u32[]{:S(2)}, u32[]{:S(2)}) collective-permute-start(f32[16,1536]{1,0:T(8,128)S(1)} %get-tuple-element.35), channel_id=1, source_target_pairs={{0,14},{1,15},{2,16},{3,17},{4,18},{5,19},{6,20},{7,21},{8,22},{9,... | collective-permute-start | bytes 294920
  4428.8 95.2 %collective-permute-start.108 = (f32[16,1536]{1,0:T(8,128)S(1)}, f32[16,1536]{1,0:T(8,128)}, u32[]{:S(2)}, u32[]{:S(2)}) collective-permute-start(f32[16,1536]{1,0:T(8,128)S(1)} %get-tuple-element.35), channel_id=1, source_target_pairs={{0,13},{1,14},{2,15},{3,16},{4,17},{5,18},{6,19},{7,20},{8,21},{9,... | collective-permute-start | bytes 294920
  4432.0 93.4 %collective-permute-start.107 = (f32[16,1536]{1,0:T(8,128)S(1)}, f32[16,1536]{1,0:T(8,128)}, u32[]{:S(2)}, u32[]{:S(2)}) collective-permute-start(f32[16,1536]{1,0:T(8,128)S(1)} %get-tuple-element.35), channel_id=1, source_target_pairs={{0,12},{1,13},{2,14},{3,15},{4,16},{5,17},{6,18},{7,19},{8,20},{9,... | collective-permute-start | bytes 294920
  4434.6 96.7 %collective-permute-start.106 = (f32[16,1536]{1,0:T(8,128)S(1)}, f32[16,1536]{1,0:T(8,128)}, u32[]{:S(2)}, u32[]{:S(2)}) collective-permute-start(f32[16,1536]{1,0:T(8,128)S(1)} %get-tuple-element.35), channel_id=1, source_target_pairs={{0,11},{1,12},{2,13},{3,14},{4,15},{5,16},{6,17},{7,18},{8,19},{9,... | collective-permute-start | bytes 294920
  4525.4 19.5 collective-permute-start.102
  4534.7 50.0 %collective-permute-start.100 = (f32[16,1536]{1,0:T(8,128)S(1)}, f32[16,1536]{1,0:T(8,128)}, u32[]{:S(2)}, u32[]{:S(2)}) collective-permute-start(f32[16,1536]{1,0:T(8,128)S(1)} %get-tuple-element.35), channel_id=1, source_target_pairs={{0,5},{1,6},{2,7},{3,8},{4,9},{5,10},{6,11},{7,12},{8,13},{9,14},{... | collective-permute-start | bytes 294920
  4537.9 46.7 %collective-permute-start.99 = (f32[16,1536]{1,0:T(8,128)S(1)}, f32[16,1536]{1,0:T(8,128)}, u32[]{:S(2)}, u32[]{:S(2)}) collective-permute-start(f32[16,1536]{1,0:T(8,128)S(1)} %get-tuple-element.35), channel_id=1, source_target_pairs={{0,4},{1,5},{2,6},{3,7},{4,8},{5,9},{6,10},{7,11},{8,12},{9,13},{1... | collective-permute-start | bytes 294920
  4542.9 41.7 collective-permute-start.98
  4544.9 39.8 collective-permute-start.97
  4547.3 37.4 collective-permute-start.96
  (428 other events, 22581.3 us)
Sparse Core Ops, SparseCore 0:
  9.7 302.8 all-gather.27
  314.4 301.4 all-gather.25
  617.5 312.1 all-gather.29
  931.2 311.9 all-gather.31
  1244.7 31.4 all-gather.19
  1277.7 78.8 all-gather.21
  1358.3 32.2 all-gather.23
  1392.3 306.1 all-gather.33
  1700.2 399.4 all-gather.35
  2101.2 314.1 all-gather.17
  2418.4 30.2 reduce-scatter.20
  2450.9 29.5 reduce-scatter.22
  2483.4 29.5 reduce-scatter.24
  2515.9 708.1 reduce-scatter.18
where the time goes:
time: 4670 us; the launch traced here: 4650 us
  waiting for transfers between devices  1780 us (38%)
  blocking collectives  1740 us (37%)
  starting transfers between devices  616 us (13%)
  local copies, waits for them, and re-layouts  335 us (7%)
  matrix products  115 us (2%)
    unnamed x3, blocking collectives  1370 us
    unnamed x224, starting transfers between devices  580 us
    all_gather x1, blocking collectives, local(): lax.all_gather(router_weight, ('fsdp', 'rep'), axis=0, tiled=True)  364 us
    all_gather x1, waiting for transfers between devices, local(): lax.all_gather(query_weight, ('fsdp', 'rep'), axis=0, tiled=True)  311 us
    all_gather x1, waiting for transfers between devices, local(): lax.all_gather(shared_down, ('fsdp', 'rep'), axis=0, tiled=True)  306 us
    all_gather x1, waiting for transfers between devices, local(): lax.all_gather(output_weight, ('fsdp', 'rep'), axis=0, tiled=True)  302 us
    all_gather x1, waiting for transfers between devices, local(): lax.all_gather(value_weight, ('fsdp', 'rep'), axis=0, tiled=True)  300 us
    unnamed x503, local copies, waits for them, and re-layouts  270 us
  transfers between devices with their start and end apart: 242, of which 10 were waited for; matrix products, arithmetic and copies ran while one was open for 37% of the time, Pallas kernels for 0%

commit v1 on v0

v1 whole, which is shorter than its diff:
```python
import functools
import math

import jax
import jax.numpy as jnp
from jax import lax
from jax.experimental import pallas as pl
from jax.experimental.pallas import tpu as pltpu
from jax.sharding import PartitionSpec as P

MESH = pl.DeviceIdType.MESH
ANY = pl.BlockSpec(memory_space=pl.ANY)
VM = pl.BlockSpec(memory_space=pltpu.VMEM)
ORDERS = ("xyz", "yzx", "zxy", "xyz", "yzx", "zxy")
PIECE = [12, 12, 12, 12, 12, 8]


def place():
    f, r = lax.axis_index("fsdp"), lax.axis_index("rep")
    return dict(x=(f // 2) % 4, y=2 * r + (f // 8) % 2, z=f // 16, core=f % 2)


def device(at):
    return (((at["z"] * 2 + at["y"] % 2) * 4 + at["x"]) * 2 + at["core"], at["y"] // 2)


def moved(at, axis, by):
    return {**at, axis: (at[axis] + by) % (2 if axis == "core" else 4)}


def region(at, order, done, coordinate=None, half=None):
    first = done[0] if done else None
    spot = {}
    for axis in "xyz":
        whole = axis in done
        at_axis = at[axis]
        if axis == "y":
            if whole:
                spot["yhi"] = (half if (half is not None and first == "y") else slice(None))
                spot["ylo"] = slice(None)
            else:
                spot["yhi"], spot["ylo"] = at_axis // 2, at_axis % 2
        else:
            if whole:
                spot[axis] = pl.ds(2 * half, 2) if (half is not None and first == axis) else slice(None)
            else:
                spot[axis] = at_axis
    return (at["core"], spot["yhi"], spot["z"], spot["ylo"], spot["x"])


def gather_kernel(*refs, n, rows, piece):
    ins, outs = refs[:n], refs[n:2 * n]
    got, stage = refs[2 * n:3 * n], refs[3 * n:4 * n]
    mix_send, mix_recv, own_sem, send, recv, dsend, drecv = refs[4 * n:]
    at = place()
    mine = at["core"] * 2 + at["y"] // 2
    peers = [moved(at, "core", 1), moved(at, "y", 2), moved(moved(at, "core", 1), "y", 2)]
    around = [moved(at, axis, by) for axis in "xyz" for by in (1, -1)]
    barrier = pltpu.get_barrier_semaphore()
    for other in peers + around:
        pl.semaphore_signal(barrier, inc=1, device_id=device(other), device_id_type=MESH)
    pl.semaphore_wait(barrier, len(peers) + len(around))

    def remote(src, dst, s, r, to):
        return pltpu.make_async_remote_copy(src_ref=src, dst_ref=dst, send_sem=s, recv_sem=r, device_id=device(to), device_id_type=MESH)

    started = []

    def go(copy):
        copy.start()
        started.append(copy)
        return copy

    mixes = []
    for i in range(n):
        own = pltpu.make_async_copy(ins[i].at[mine], got[i].at[mine], own_sem.at[i])
        own.start()
        copies = []
        for k, to in enumerate(peers):
            quarter = to["core"] * 2 + to["y"] // 2
            copies.append(go(remote(ins[i].at[quarter], got[i].at[mine], mix_send.at[i, k], mix_recv.at[i, k], to)))
        mixes.append((own, copies))
    keep = []
    for i in range(n):
        own, copies = mixes[i]
        own.wait()
        for copy in copies:
            copy.wait_recv()
        size, take = rows[i], piece[i]
        to_row = lax.broadcasted_iota(jnp.int32, (size, 64), 0)
        from_row = lax.broadcasted_iota(jnp.int32, (size, 64), 1)
        pick = ((to_row // take) * 16 + to_row % take == from_row).astype(jnp.bfloat16)
        whole = got[i][...].reshape(64, got[i].shape[2])
        stage[i][...] = jnp.dot(pick, whole, preferred_element_type=jnp.float32).astype(jnp.bfloat16)
        local = pltpu.make_async_copy(stage[i], outs[i].at[region(at, ORDERS[i], "")], own_sem.at[i])
        local.start()
        keep.append(local)
    sibling = moved(at, "core", 1)
    for phase in range(3):
        firsts, seconds = [], []
        if phase == 1:
            for local in keep:
                local.wait()
        for i in range(n):
            order = ORDERS[i]
            axis, done = order[phase], order[:phase]
            here = region(at, order, done)
            src = stage[i] if phase == 0 else outs[i].at[here]
            up = go(remote(src, outs[i].at[here], send.at[i, phase, 0], recv.at[i, phase, 0], moved(at, axis, 1)))
            down = go(remote(src, outs[i].at[here], send.at[i, phase, 1], recv.at[i, phase, 1], moved(at, axis, -1)))
            firsts.append((up, down))
            if phase == 0:
                go(remote(src, outs[i].at[here], dsend.at[i, 0, 4], drecv.at[i, 0, 4], sibling))
        for i in range(n):
            order = ORDERS[i]
            axis, done = order[phase], order[:phase]
            up, down = firsts[i]
            pair = []
            for k, (copy, step) in enumerate(((up, 1), (down, -1))):
                copy.wait_recv()
                block = moved(at, axis, -step)
                if phase == 0:
                    low = 16 if rows[i] == 48 else rows[i] // 2
                    part = pl.ds(0, low) if k == 0 else pl.ds(low, rows[i] - low)
                    where = region(block, order, done) + (part,)
                else:
                    where = region(block, order, done, half=k)
                pair.append(go(remote(outs[i].at[where], outs[i].at[where], send.at[i, phase, 2 + k], recv.at[i, phase, 2 + k], moved(at, axis, step))))
                whole = region(block, order, done)
                go(remote(outs[i].at[whole], outs[i].at[whole], dsend.at[i, phase, k], drecv.at[i, phase, k], sibling))
            seconds.append(pair)
        for i in range(n):
            order = ORDERS[i]
            axis, done = order[phase], order[:phase]
            for k in range(2):
                seconds[i][k].wait_recv()
            far = region(moved(at, axis, 2), order, done)
            go(remote(outs[i].at[far], outs[i].at[far], dsend.at[i, phase, 2], drecv.at[i, phase, 2], sibling))
    for copy in started:
        copy.wait_send()
    for i in range(n):
        order = ORDERS[i]
        for phase in range(3):
            axis, done = order[phase], order[:phase]
            for k, by in enumerate((-1, 1, 2)):
                there = moved(moved(at, axis, by), "core", 1)
                where = outs[i].at[region(there, order, done)]
                remote(where, where, dsend.at[i, phase, k], drecv.at[i, phase, k], sibling).wait_recv()
        where = outs[i].at[region(sibling, order, "")]
        remote(where, where, dsend.at[i, 0, 4], drecv.at[i, 0, 4], sibling).wait_recv()


def gather(shards, piece, cid=1):
    n = len(shards)
    rows = [4 * p for p in piece]
    outs = pl.pallas_call(
        functools.partial(gather_kernel, n=n, rows=rows, piece=piece),
        out_shape=[jax.ShapeDtypeStruct((2, 2, 4, 2, 4, rows[i], shards[i].shape[2]), jnp.bfloat16) for i in range(n)],
        in_specs=[VM] * n,
        out_specs=[ANY] * n,
        scratch_shapes=[pltpu.VMEM((4, 16, s.shape[2]), jnp.bfloat16) for s in shards]
        + [pltpu.VMEM((rows[i], shards[i].shape[2]), jnp.bfloat16) for i in range(n)]
        + [pltpu.SemaphoreType.DMA((n, 3)), pltpu.SemaphoreType.DMA((n, 3)), pltpu.SemaphoreType.DMA((n,)),
           pltpu.SemaphoreType.DMA((n, 3, 4)), pltpu.SemaphoreType.DMA((n, 3, 4)),
           pltpu.SemaphoreType.DMA((n, 3, 5)), pltpu.SemaphoreType.DMA((n, 3, 5))],
        compiler_params=pltpu.CompilerParams(collective_id=cid, has_side_effects=True, vmem_limit_bytes=40 << 20),
        name="gather_weights",
    )(*shards)
    return [o.reshape(4, 32 * rows[i], o.shape[-1]) for i, o in enumerate(outs)]


def pack(local, piece):
    p, n = local.shape
    q = local.reshape(p, 4, n // 4).transpose(1, 0, 2)
    return jnp.pad(q, ((0, 0), (0, 16 - p), (0, 0)))


def half_shape(order, phase):
    if phase == 0:
        return ()
    if phase == 1:
        return (2,)
    return {"xyz": (2, 2, 2), "yzx": (4, 2), "zxy": (2, 4)}[order]


def scatter_kernel(*refs, n, rows, piece, orders):
    ins, outs = refs[:n], refs[n:2 * n]
    total, other = refs[2 * n:3 * n], refs[3 * n:4 * n]
    landing = [refs[4 * n + 3 * i:4 * n + 3 * i + 3] for i in range(n)]
    spread = refs[7 * n:8 * n]
    own_sem, dsend, drecv, send, recv, msend, mrecv = refs[8 * n:]
    at = place()
    mine = at["core"] * 2 + at["y"] // 2
    sibling = moved(at, "core", 1)
    peers = [sibling, moved(at, "y", 2), moved(sibling, "y", 2)]
    around = [moved(at, axis, by) for axis in "xyz" for by in (1, -1)]
    barrier = pltpu.get_barrier_semaphore()
    for to in peers + around:
        pl.semaphore_signal(barrier, inc=1, device_id=device(to), device_id_type=MESH)
    pl.semaphore_wait(barrier, len(peers) + len(around))

    def remote(src, dst, s, r, to):
        return pltpu.make_async_remote_copy(src_ref=src, dst_ref=dst, send_sem=s, recv_sem=r, device_id=device(to), device_id_type=MESH)

    started = []

    def go(copy):
        copy.start()
        started.append(copy)
        return copy

    def add(to, where, ref, spot):
        to[where] = (to[where].astype(jnp.float32) + ref[spot].astype(jnp.float32)).astype(jnp.bfloat16)

    firsts = []
    for i in range(n):
        own = pltpu.make_async_copy(ins[i].at[at["core"]], total[i], own_sem.at[i])
        own.start()
        firsts.append((own, go(remote(ins[i].at[1 - at["core"]], other[i], dsend.at[i], drecv.at[i], sibling))))

    def cut(i, k):
        low = 16
        return pl.ds(0, low) if k == 0 else pl.ds(low, rows[i] - low)

    def part(i, phase, spot, k):
        done = orders[i][:phase]
        if phase == 0:
            return region(spot, orders[i], done)[1:] + (cut(i, k),)
        return region(spot, orders[i], done, half=k)[1:]

    def box(i, phase, side, k, message):
        ref = landing[i][phase]
        if phase == 0:
            return (side, message, cut(i, k))
        return (side, message)

    def message(i, phase, side, number):
        axis = orders[i][phase]
        step = 1 if side == 0 else -1
        spot, k = ((moved(at, axis, 2), side), (moved(at, axis, step), 1 - side), (moved(at, axis, step), side))[number]
        src = total[i].at[part(i, phase, spot, k)]
        dst = landing[i][phase].at[box(i, phase, side, k, number)]
        return remote(src, dst, send.at[i, phase, side, number], recv.at[i, phase, side, number], moved(at, axis, step))

    sent = {}
    for i in range(n):
        own, copy = firsts[i]
        own.wait()
        copy.wait_recv()

        def both(z, carry, i=i):
            for h in range(2):
                for l in range(2):
                    for x in range(4):
                        add(total[i], (h, z, l, x), other[i], (h, z, l, x))
            return carry
        lax.fori_loop(0, 4, both, 0)
        for number in range(2):
            for side in range(2):
                sent[i, 2, side, number] = go(message(i, 2, side, number))
    for phase in (2, 1, 0):
        for i in range(n):
            axis = orders[i][phase]
            for side in range(2):
                step = 1 if side == 0 else -1
                sent[i, phase, side, 0].wait_recv()
                add(total[i], part(i, phase, moved(at, axis, step), side), landing[i][phase], box(i, phase, side, side, 0))
                sent[i, phase, side, 2] = go(message(i, phase, side, 2))
        for i in range(n):
            for side in range(2):
                for number in (1, 2):
                    sent[i, phase, side, number].wait_recv()
            if phase > 0:
                for side in range(2):
                    add(total[i], part(i, phase, at, 1 - side), landing[i][phase], box(i, phase, side, 1 - side, 1))
                    add(total[i], part(i, phase, at, side), landing[i][phase], box(i, phase, side, side, 2))
                for number in range(2):
                    for side in range(2):
                        sent[i, phase - 1, side, number] = go(message(i, phase - 1, side, number))
            else:
                here = region(at, orders[i], "")[1:]
                def rows_of(k):
                    s = cut(i, k)
                    whole = total[i][here + (s,)].astype(jnp.float32)
                    for side in range(2):
                        whole = whole + landing[i][0][box(i, 0, side, k, 1 if k == 1 - side else 2)].astype(jnp.float32)
                    return whole
                chunk = jnp.concatenate([rows_of(0), rows_of(1)], axis=0).astype(jnp.bfloat16)
                size, take = rows[i], piece[i]
                to_row = lax.broadcasted_iota(jnp.int32, (64, size), 0)
                from_row = lax.broadcasted_iota(jnp.int32, (64, size), 1)
                pick = ((from_row // take) * 16 + from_row % take == to_row).astype(jnp.bfloat16)
                laid = jnp.dot(pick, chunk, preferred_element_type=jnp.float32).astype(jnp.bfloat16)
                spread[i][...] = laid.reshape(4, 16, laid.shape[-1])
                own = pltpu.make_async_copy(spread[i].at[mine], outs[i].at[mine], own_sem.at[i])
                own.start()
                finals = [own]
                for k, to in enumerate(peers):
                    quarter = to["core"] * 2 + to["y"] // 2
                    finals.append(go(remote(spread[i].at[quarter], outs[i].at[mine], msend.at[i, k], mrecv.at[i, k], to)))
                sent[i, "final"] = finals
    for i in range(n):
        own, *copies = sent[i, "final"]
        own.wait()
        for copy in copies:
            copy.wait_recv()
    for copy in started:
        copy.wait_send()


def scatter(parts, piece, orders, cid=2):
    n = len(parts)
    rows = [4 * p for p in piece]
    wide = [p.shape[-1] for p in parts]
    ins = [p.reshape(2, 2, 4, 2, 4, rows[i], wide[i]) for i, p in enumerate(parts)]
    scratch = [pltpu.VMEM((2, 4, 2, 4, rows[i], wide[i]), jnp.bfloat16) for i in range(n)] * 2
    for i in range(n):
        for phase in range(3):
            scratch.append(pltpu.VMEM((2, 3) + half_shape(orders[i], phase) + (rows[i], wide[i]), jnp.bfloat16))
    scratch += [pltpu.VMEM((4, 16, wide[i]), jnp.bfloat16) for i in range(n)]
    dma = pltpu.SemaphoreType.DMA
    scratch += [dma((n,)), dma((n,)), dma((n,)), dma((n, 3, 2, 3)), dma((n, 3, 2, 3)), dma((n, 3)), dma((n, 3))]
    return pl.pallas_call(
        functools.partial(scatter_kernel, n=n, rows=rows, piece=piece, orders=orders),
        out_shape=[jax.ShapeDtypeStruct((4, 16, w), jnp.bfloat16) for w in wide],
        in_specs=[ANY] * n,
        out_specs=[VM] * n,
        scratch_shapes=scratch,
        compiler_params=pltpu.CompilerParams(collective_id=cid, has_side_effects=True, vmem_limit_bytes=56 << 20),
        name="scatter_grads",
    )(*ins)


def unpack(out, piece):
    return out[:, :piece].transpose(1, 0, 2).reshape(piece, -1).astype(jnp.float32)


D = 1536
TOK = 128
TOP = 6
EXPERTS = 64
CAP = 24
SLOTS = EXPERTS * CAP
CHUNK = 384
epsilon = 1e-06
SCALE = 1.0 / math.sqrt(128)
f32, bf16, i32 = jnp.float32, jnp.bfloat16, jnp.int32


def dot(a, b):
    return jnp.dot(a, b, preferred_element_type=f32)


def dot_t(a, b):
    return lax.dot_general(a, b, (((1,), (1,)), ((), ())), preferred_element_type=f32)


def t_dot(a, b):
    return lax.dot_general(a, b, (((0,), (0,)), ((), ())), preferred_element_type=f32)


def flip(a):
    return a.astype(f32).T.astype(bf16)


def rms_scale(v):
    return lax.rsqrt(jnp.mean(v * v, axis=-1, keepdims=True) + epsilon)


def silu_parts(pre):
    s = jax.nn.sigmoid(pre)
    return pre * s, s * (1.0 + pre * (1.0 - s))


def norm_back(grad, source, scale, gain):
    weighted = grad * gain
    inner = jnp.mean(weighted * source, axis=-1, keepdims=True)
    return scale * weighted - source * (scale * scale * scale) * inner


def iota(shape, dim):
    return lax.broadcasted_iota(i32, shape, dim)


def gain_row(misc, lane):
    pick = (iota((16, 128), 1) == lane).astype(bf16)
    return dot_t(pick, misc)[0:1]


def chosen(routes):
    lanes = iota((TOK, 128), 1)
    hit = jnp.zeros((TOK, 128), f32)
    for k in range(TOP):
        hit = hit + (routes[:, k : k + 1] == lanes).astype(f32)
    return hit


def attend_body(tokens, seg, routes, wq, wkv, wo, normed_o, q_o, kv_o, p_o, att_o, resid_o, nt_o, code_o):
    source = tokens[...].astype(f32)
    gain = gain_row(wkv[0, :, 256:], 64)
    normed_o[...] = (source * rms_scale(source) * gain).astype(bf16)
    row = jnp.broadcast_to(seg[...].astype(f32), (TOK, TOK))
    allowed = (row == row.T) & (iota((TOK, TOK), 1) <= iota((TOK, TOK), 0))
    allowed = jnp.concatenate([allowed.astype(f32)] * 3, axis=0)

    def heads(j, carry):
        normed = normed_o[...]
        q = dot(normed, wq[j]).astype(bf16)
        kv = dot(normed, wkv[j, :, :256]).astype(bf16)
        q_o[j] = q
        kv_o[j] = kv
        q3 = jnp.concatenate([q[:, :128], q[:, 128:256], q[:, 256:]], axis=0)
        scores = jnp.where(allowed > 0, dot_t(q3, kv[:, :128]) * SCALE, -1e30)
        expo = jnp.exp(scores - jnp.max(scores, axis=-1, keepdims=True))
        p = expo / jnp.sum(expo, axis=-1, keepdims=True)
        p_o[j] = p
        mixed = dot(p.astype(bf16), kv[:, 128:]).astype(bf16)
        att_o[j] = jnp.concatenate([mixed[:128], mixed[128:256], mixed[256:]], axis=1)
        return carry

    lax.fori_loop(0, 4, heads, 0)
    attended = jnp.concatenate([att_o[j] for j in range(4)], axis=1)
    for j in range(4):
        resid_o[:, j * 384 : (j + 1) * 384] = source[:, j * 384 : (j + 1) * 384] + dot(attended, wo[j])
    resid = resid_o[...]
    nt = (resid * rms_scale(resid) * gain_row(wkv[0, :, 256:], 65)).astype(bf16)
    nt_o[...] = nt
    logits = dot(nt, wkv[0, :, 256:])
    hit = chosen(routes[...])
    earlier = (iota((TOK, TOK), 1) < iota((TOK, TOK), 0)).astype(bf16)
    code_o[0] = hit * (dot(earlier, hit.astype(bf16)) + 1.0)
    masked = jnp.where(hit > 0, logits, -1e30)
    expo = jnp.where(hit > 0, jnp.exp(masked - jnp.max(masked, axis=-1, keepdims=True)), 0.0)
    code_o[1] = expo / jnp.sum(expo, axis=-1, keepdims=True)


def back_body(gnt, resid_r, cot, tokens, normed_r, q_r, kv_r, p_r, att_r, wq, wkv, wo, misc_in, gtok_o, gwq_o, gwkv_o, gwo_o, gq_s, gkv_s, goo_s, gatt_s, nt_s):
    total = gnt[...]
    resid = resid_r[...]
    scale = rms_scale(resid)
    z_two = (total * resid * scale).astype(bf16)
    grad_resid = cot[...].astype(f32) + norm_back(total, resid, scale, gain_row(wkv[0, :, 256:], 65))
    goo_s[...] = grad_resid.astype(bf16)
    att_t = flip(jnp.concatenate([att_r[j] for j in range(4)], axis=1))
    gatt = jnp.zeros((TOK, D), f32)
    for j in range(4):
        cols = slice(j * 384, (j + 1) * 384)
        gatt = gatt + dot_t(goo_s[:, cols], wo[j])
        gwo_o[j] = dot(att_t, goo_s[:, cols]).astype(bf16)
    for j in range(4):
        gatt_s[j] = gatt[:, j * 384 : (j + 1) * 384].astype(bf16)

    def heads(j, carry):
        ga, q, kv, p = gatt_s[j], q_r[j], kv_r[j], p_r[j]
        ga3 = jnp.concatenate([ga[:, :128], ga[:, 128:256], ga[:, 256:]], axis=0)
        q3 = jnp.concatenate([q[:, :128], q[:, 128:256], q[:, 256:]], axis=0)
        gp = dot_t(ga3, kv[:, 128:])
        gs = (p * (gp - jnp.sum(p * gp, axis=-1, keepdims=True))).astype(bf16)
        gq3 = (dot(gs, kv[:, :128]) * SCALE).astype(bf16)
        gk = (t_dot(gs, q3) * SCALE).astype(bf16)
        gv = t_dot(p.astype(bf16), ga3).astype(bf16)
        gq_s[j] = jnp.concatenate([gq3[:128], gq3[128:256], gq3[256:]], axis=1)
        gkv_s[j] = jnp.concatenate([gk, gv], axis=1)
        return carry

    lax.fori_loop(0, 4, heads, 0)
    nt_s[...] = flip(normed_r[...])
    gn = jnp.zeros((TOK, D), f32)
    for j in range(4):
        gn = gn + dot_t(gq_s[j], wq[j]) + dot_t(gkv_s[j], wkv[j, :, :256])
        gwq_o[j] = dot(nt_s[...], gq_s[j]).astype(bf16)
        gwkv_o[j, :, :256] = dot(nt_s[...], gkv_s[j]).astype(bf16)
        if j:
            gwkv_o[j, :, 256:] = jnp.zeros((D, 128), bf16)
    source = tokens[...].astype(f32)
    scale = rms_scale(source)
    z_one = (gn * source * scale).astype(bf16)
    gtok_o[...] = grad_resid + norm_back(gn, source, scale, gain_row(wkv[0, :, 256:], 64))
    lane = iota((TOK, 128), 1)
    gwkv_o[0, :, 256:] = (misc_in[...] + t_dot(z_one, (lane == 64).astype(bf16)) + t_dot(z_two, (lane == 65).astype(bf16))).astype(bf16)


def sds(shape, dtype=bf16):
    return jax.ShapeDtypeStruct(shape, dtype)


def whole(body, outs, scratch=(), name=None):
    def call(*args):
        return pl.pallas_call(
            body,
            out_shape=outs,
            in_specs=[pl.BlockSpec(memory_space=pltpu.VMEM)] * len(args),
            out_specs=[pl.BlockSpec(memory_space=pltpu.VMEM)] * len(outs),
            scratch_shapes=[pltpu.VMEM(s.shape, s.dtype) for s in scratch],
            compiler_params=pltpu.CompilerParams(vmem_limit_bytes=60 << 20),
            name=name,
        )(*args)

    return call


attend = whole(
    attend_body,
    [sds((TOK, D)), sds((4, TOK, 384)), sds((4, TOK, 256)), sds((4, 384, TOK), f32), sds((4, TOK, 384)), sds((TOK, D), f32), sds((TOK, D)), sds((2, TOK, 128), f32)],
    name="attend",
)
back = whole(
    back_body,
    [sds((TOK, D), f32), sds((4, D, 384)), sds((4, D, 384)), sds((4, D, 384))],
    [sds((4, TOK, 384)), sds((4, TOK, 256)), sds((TOK, D)), sds((4, TOK, 384)), sds((D, TOK))],
    name="back",
)


STRIDE = 11
PEERS = 32
BLOCK = 2 * CAP
GROUP = CHUNK // BLOCK


def shift_of(s):
    t = (s * STRIDE) % PEERS
    return t // 8, (t // 2) % 4, t % 2


def shifted(at, s, sign):
    dz, dx, dc = shift_of(s)
    return {
        **at,
        "z": (at["z"] + sign * dz + 4) % 4,
        "x": (at["x"] + sign * dx + 4) % 4,
        "core": (at["core"] + dc) % 2,
    }


def moe_kernel(
    nt_h, cot_h, code_r, resid_h, router_r, gm, um, dm, sg_h, su_h, sd_h,
    out_r, gnt_r, misc_r, gg_o, gu_o, gd_o, gsg_h, gsu_h, gsd_h,
    nt2, cot2, code2, hits, gated, owner, out_n, out_g, arr_n, arr_g, ret_m, ret_b,
    gx, ux, dx, hid, act_s, slope_s, acc, grecv_a, grecv_b, part_s, part_r, pick_s, pick_r,
    sg_v, su_v, sd_v, shid, ntt, stage,
    pair_send, pair_recv, rep_send, rep_recv, n_send, n_recv, g_send, g_recv, m_send, m_recv, b_send, b_recv, self_sem, load_sem, store_sem,
):
    at = place()
    partner = {**at, "y": at["y"] + 1 - 2 * (at["y"] % 2)}
    twin = moved(at, "y", 2)
    barrier = pltpu.get_barrier_semaphore()
    for to in (partner, twin):
        pl.semaphore_signal(barrier, inc=1, device_id=device(to), device_id_type=MESH)

    def hello(s, carry):
        pl.semaphore_signal(barrier, inc=1, device_id=device(shifted(at, s, 1)), device_id_type=MESH)
        return carry

    lax.fori_loop(1, PEERS, hello, 0)
    pl.semaphore_wait(barrier, PEERS + 1)

    def remote(src, dst, s, r, to):
        return pltpu.make_async_remote_copy(src_ref=src, dst_ref=dst, send_sem=s, recv_sem=r, device_id=device(to), device_id_type=MESH)

    started = []

    def go(copy):
        copy.start()
        started.append(copy)
        return copy

    nt_r, cot = nt2.at[0], cot2.at[0]
    first = [pltpu.make_async_copy(nt_h, nt_r, load_sem.at[5]), pltpu.make_async_copy(cot_h, cot, load_sem.at[6])]
    for copy in first:
        copy.start()
    pair = [go(remote(src, dst, pair_send.at[k], pair_recv.at[k], partner)) for k, (src, dst) in enumerate(((nt_h, nt2.at[1]), (code_r, code2), (cot_h, cot2.at[1])))]
    swaps = [go(remote(src, dst, rep_send.at[k], rep_recv.at[k], twin)) for k, (src, dst) in enumerate(((gm, gx), (um, ux), (dm, dx)))]

    def load(src, dst, k):
        copy = pltpu.make_async_copy(src, dst, load_sem.at[k])
        copy.start()
        return copy

    sd_copy = load(sd_h, sd_v, 4)
    loads = {}
    for j in range(2):
        loads[j] = (load(sg_h.at[j], sg_v.at[j], j), load(su_h.at[j], su_v.at[j], 2 + j))
    lane = iota((1, SLOTS), 1)
    block, spot = lane // BLOCK, lane % BLOCK
    there = shifted(at, block, 1)
    expert = ((there["z"] * 2 + at["y"] % 2) * 4 + there["x"]) * 2 + there["core"]
    owner[...] = (iota((128, SLOTS), 0) == expert).astype(bf16)
    for copy in first:
        copy.wait()
    ntt[...] = flip(nt_r[...])

    def fill(k, code, gates):
        wide = dot(code.astype(bf16), owner[...])
        hit = (wide == (spot - k * CAP + 1).astype(f32)) & (wide > 0)
        rows = slice(k * TOK, (k + 1) * TOK)
        hits[rows] = hit.astype(f32).astype(bf16)
        gated[rows] = jnp.where(hit, dot(gates.astype(bf16), owner[...]), 0.0).astype(bf16)

    fill(0, code_r[0], code_r[1])
    for copy in pair[:2]:
        copy.wait_recv()
    fill(1, code2[0], code2[1])

    def send_rows(box, land, c, ssem, rsem, sign):
        def one(s, carry):
            remote(box.at[s], land.at[s], ssem.at[s], rsem.at[s], shifted(at, s, sign)).start()
            return carry
        if c == 0:
            pltpu.make_async_copy(box.at[0], land.at[0], self_sem).start()
        lax.fori_loop(max(1, c * GROUP), (c + 1) * GROUP, one, 0)

    def wait_rows(box, land, c, ssem, rsem, sign, sent):
        def one(s, carry):
            copy = remote(box.at[s], land.at[s], ssem.at[s], rsem.at[s], shifted(at, s, sign))
            if sent:
                copy.wait_send()
            else:
                copy.wait_recv()
            return carry
        if c == 0 and not sent:
            pltpu.make_async_copy(box.at[0], land.at[0], self_sem).wait()
        lax.fori_loop(max(1, c * GROUP), (c + 1) * GROUP, one, 0)

    chunks = range(SLOTS // CHUNK)

    def lanes_of(c):
        return slice(c * CHUNK, (c + 1) * CHUNK)

    def blocks_of(c):
        return slice(c * GROUP, (c + 1) * GROUP)

    for c in chunks:
        rows = t_dot(hits[:, lanes_of(c)], nt2[...].reshape(2 * TOK, D))
        out_n[blocks_of(c)] = rows.astype(bf16).reshape(GROUP, BLOCK, D)
        send_rows(out_n, arr_n, c, n_send, n_recv, 1)
    wait_rows(out_n, arr_n, 0, n_send, n_recv, 1, False)
    pair[2].wait_recv()
    for c in chunks:
        rows = t_dot(gated[:, lanes_of(c)], cot2[...].reshape(2 * TOK, D))
        out_g[blocks_of(c)] = rows.astype(bf16).reshape(GROUP, BLOCK, D)
        send_rows(out_g, arr_g, c, g_send, g_recv, 1)

    sd_copy.wait()
    gh = jnp.zeros((TOK, 1024), f32)
    for j in range(4):
        gh = gh + dot_t(cot[:, j * 384 : (j + 1) * 384], sd_v[j])
    stores = []

    def store(k, value, dst):
        while len(stores) >= 2:
            stores.pop(0).wait()
        stage[k % 2] = value.astype(bf16)
        copy = pltpu.make_async_copy(stage.at[k % 2], dst, store_sem.at[k % 2])
        copy.start()
        stores.append(copy)

    acc[...] = jnp.zeros((2 * TOK, D), f32)
    for j in range(4):
        for copy in loads[j]:
            copy.wait()
        cols = slice(j * 256, (j + 1) * 256)
        gate, up = dot(nt_r[...], sg_v[j % 2]), dot(nt_r[...], su_v[j % 2])
        act, slope = silu_parts(gate)
        shid[:, cols] = (act * up).astype(bf16)
        dgate = (gh[:, cols] * up * slope).astype(bf16)
        dup = (gh[:, cols] * act).astype(bf16)
        acc[:TOK] += dot_t(dgate, sg_v[j % 2]) + dot_t(dup, su_v[j % 2])
        if j < 2:
            loads[j + 2] = (load(sg_h.at[j + 2], sg_v.at[j], j), load(su_h.at[j + 2], su_v.at[j], 2 + j))
        store(2 * j, dot(ntt[...], dgate), gsg_h.at[j])
        store(2 * j + 1, dot(ntt[...], dup), gsu_h.at[j])
    gnt_r[...] = acc[:TOK]
    resid_copy = load(resid_h, acc.at[pl.ds(0, TOK)], 5)
    for copy in stores:
        copy.wait()
    stores.clear()
    shid_t = flip(shid[...])
    finals = []
    resid_copy.wait()
    for j in range(4):
        cols = slice(j * 384, (j + 1) * 384)
        acc[:TOK, cols] += dot(shid[...], sd_v[j])
    acc[TOK:] = jnp.zeros((TOK, D), f32)
    for j in range(4):
        sd_v[j] = dot(shid_t, cot[:, j * 384 : (j + 1) * 384]).astype(bf16)
        copy = pltpu.make_async_copy(sd_v.at[j], gsd_h.at[j], load_sem.at[j])
        copy.start()
        finals.append(copy)

    for copy in swaps:
        copy.wait_recv()
    halves = ((gm, um, dm), (gx, ux, dx))
    for c in chunks:
        if c:
            wait_rows(out_n, arr_n, c, n_send, n_recv, 1, False)
        x = arr_n[blocks_of(c)].reshape(CHUNK, D)
        total = None
        for k, (g, u, d) in enumerate(halves):
            cols = slice(k * 256, (k + 1) * 256)
            gate, up = dot(x, g[...]), dot(x, u[...])
            act, slope = silu_parts(gate)
            hidden = (act * up).astype(bf16)
            hid[lanes_of(c), cols] = hidden
            act_s[lanes_of(c), cols] = act.astype(bf16)
            slope_s[lanes_of(c), cols] = (up * slope).astype(bf16)
            part = dot(hidden, d[...])
            total = part if total is None else total + part
        wait_rows(out_n, arr_n, c, n_send, n_recv, 1, True)
        out_n[blocks_of(c)] = total.astype(bf16).reshape(GROUP, BLOCK, D)
        send_rows(out_n, ret_m, c, m_send, m_recv, -1)
    wait_rows(out_n, ret_m, 0, m_send, m_recv, -1, False)
    send_self = None
    for c in chunks:
        wait_rows(out_g, arr_g, c, g_send, g_recv, 1, False)
        slot = arr_g[blocks_of(c)].reshape(CHUNK, D)
        total = None
        for k, (g, u, d) in enumerate(halves):
            cols = slice(k * 256, (k + 1) * 256)
            gh = dot_t(slot, d[...])
            dgate = (gh * slope_s[lanes_of(c), cols].astype(f32)).astype(bf16)
            dup = (gh * act_s[lanes_of(c), cols].astype(f32)).astype(bf16)
            slope_s[lanes_of(c), cols], act_s[lanes_of(c), cols] = dgate, dup
            part = dot_t(dgate, g[...]) + dot_t(dup, u[...])
            total = part if total is None else total + part
        wait_rows(out_g, arr_g, c, g_send, g_recv, 1, True)
        out_g[blocks_of(c)] = total.astype(bf16).reshape(GROUP, BLOCK, D)
        send_rows(out_g, ret_b, c, b_send, b_recv, -1)
    for b in range(4):
        cols = slice(b * 384, (b + 1) * 384)
        xt = flip(jnp.concatenate([arr_n[blocks_of(c), :, cols].reshape(CHUNK, 384) for c in chunks], axis=0))
        gg = dot(xt, slope_s[...])
        gu = dot(xt, act_s[...])
        gg_o[cols], gu_o[cols] = gg[:, :256], gu[:, :256]
        sg_v[0, cols], sg_v[1, cols] = gg[:, 256:].astype(bf16), gu[:, 256:].astype(bf16)
    trade = [go(remote(sg_v, grecv_a, rep_send.at[3], rep_recv.at[3], twin))]
    for copy in finals:
        copy.wait()
    hid_t = flip(hid[...])
    for b in range(4):
        cols = slice(b * 384, (b + 1) * 384)
        gd = dot(hid_t, jnp.concatenate([arr_g[blocks_of(c), :, cols].reshape(CHUNK, 384) for c in chunks], axis=0))
        gd_o[:, cols] = gd[:256]
        sd_v[0, b * 256 : (b + 1) * 256] = gd[256:].astype(bf16)
    trade.append(go(remote(sd_v.at[0], grecv_b, rep_send.at[4], rep_recv.at[4], twin)))

    picked = jnp.zeros((2 * TOK, 128), f32)
    for c in chunks:
        if c:
            wait_rows(out_n, ret_m, c, m_send, m_recv, -1, False)
        rows = ret_m[blocks_of(c)].reshape(CHUNK, D)
        acc[...] += dot(gated[:, lanes_of(c)], rows)
        grads = dot_t(cot2[...].reshape(2 * TOK, D), rows) * hits[:, lanes_of(c)].astype(f32)
        high = grads.astype(bf16)
        low = (grads - high.astype(f32)).astype(bf16)
        own = owner[:, lanes_of(c)]
        picked = picked + dot_t(high, own) + dot_t(low, own)
    part_s[0] = acc[TOK:].astype(bf16)
    pick_s[...] = picked[TOK:]
    pair.append(go(remote(part_s.at[0], part_r.at[0], pair_send.at[3], pair_recv.at[3], partner)))
    pair.append(go(remote(pick_s, pick_r, pair_send.at[4], pair_recv.at[4], partner)))
    pair[3].wait_recv()
    out_r[...] = (acc[:TOK] + part_r[0].astype(f32)).astype(bf16)
    pair[4].wait_recv()
    picked = picked[:TOK] + pick_r[...]
    gates = code_r[1]
    mean = jnp.sum(gates * picked, axis=-1, keepdims=True)
    gl = (gates * (picked - mean)).astype(bf16)
    misc_r[...] = dot(ntt[...], gl)
    acc[:TOK] = gnt_r[...] + dot_t(gl, router_r[...])
    acc[TOK:] = jnp.zeros((TOK, D), f32)
    for c in chunks:
        wait_rows(out_g, ret_b, c, b_send, b_recv, -1, False)
        acc[...] += dot(hits[:, lanes_of(c)], ret_b[blocks_of(c)].reshape(CHUNK, D))
    part_s[1] = acc[TOK:].astype(bf16)
    pair.append(go(remote(part_s.at[1], part_r.at[1], pair_send.at[5], pair_recv.at[5], partner)))
    trade[0].wait_recv()
    gg_o[...] += grecv_a[0].astype(f32)
    gu_o[...] += grecv_a[1].astype(f32)
    trade[1].wait_recv()
    for b in range(4):
        gd_o[:, b * 384 : (b + 1) * 384] += grecv_b[b * 256 : (b + 1) * 256].astype(f32)
    pair[5].wait_recv()
    gnt_r[...] = acc[:TOK] + part_r[1].astype(f32)
    for c in chunks:
        wait_rows(out_n, ret_m, c, m_send, m_recv, -1, True)
        wait_rows(out_g, ret_b, c, b_send, b_recv, -1, True)
    for copy in started:
        copy.wait_send()


def moe(nt, cot, code, resid, router, mine, sg, su, sd):
    dma = pltpu.SemaphoreType.DMA
    vm = lambda shape, dtype=bf16: pltpu.VMEM(shape, dtype)
    rows = (PEERS, BLOCK, D)
    return pl.pallas_call(
        moe_kernel,
        out_shape=[sds((TOK, D)), sds((TOK, D), f32), sds((D, 128), f32), sds((D, 256), f32), sds((D, 256), f32), sds((256, D), f32), sds((4, D, 256)), sds((4, D, 256)), sds((4, 1024, 384))],
        in_specs=[ANY, ANY, VM, ANY, VM, VM, VM, VM, ANY, ANY, ANY],
        out_specs=[VM] * 6 + [ANY] * 3,
        scratch_shapes=[vm((2, TOK, D)), vm((2, TOK, D)), vm((2, TOK, 128), f32), vm((2 * TOK, SLOTS)), vm((2 * TOK, SLOTS)), vm((128, SLOTS))]
        + [vm(rows)] * 6
        + [vm((D, 256)), vm((D, 256)), vm((256, D)), vm((SLOTS, 512)), vm((SLOTS, 512)), vm((SLOTS, 512)), vm((2 * TOK, D), f32)]
        + [vm((2, D, 256)), vm((1024, 384)), vm((2, TOK, D)), vm((2, TOK, D)), vm((TOK, 128), f32), vm((TOK, 128), f32)]
        + [vm((2, D, 256)), vm((2, D, 256)), vm((4, 1024, 384)), vm((TOK, 1024)), vm((D, TOK)), vm((2, D, 256))]
        + [dma((6,)), dma((6,)), dma((5,)), dma((5,))] + [dma((PEERS,))] * 8 + [dma, dma((7,)), dma((2,))],
        compiler_params=pltpu.CompilerParams(collective_id=3, has_side_effects=True, vmem_limit_bytes=63 << 20),
        name="moe",
    )(nt, cot, code, resid, router, *mine, sg, su, sd)


def local(tokens, segment_ids, routes, cotangent, query_weight, key_weight, value_weight, output_weight, shared_gate, shared_up, shared_down, router_weight, first_gain, second_gain, expert_gate, expert_up, expert_down):
    misc = jnp.concatenate([router_weight, first_gain[:, None], second_gain[:, None], jnp.zeros((12, 62), bf16)], axis=1)
    kvm = jnp.concatenate([key_weight.reshape(12, 4, 128), value_weight.reshape(12, 4, 128), jnp.broadcast_to(misc[:, None], (12, 4, 128))], axis=2)
    wq, wo, wkv, sg, su, sd = gather(
        [pack(query_weight, 12), pack(output_weight, 12), pack(kvm.reshape(12, D), 12), pack(shared_gate, 12), pack(shared_up, 12), pack(shared_down, 8)], PIECE)
    normed, q, kv, p, att, resid, nt, code = attend(tokens, segment_ids, routes, wq, wkv, wo)
    mine = [expert_gate[0], expert_up[0], expert_down[0]]
    block_out, gnt, gmisc, gg, gu, gd, *shared_grads = moe(nt, cotangent, code, resid, wkv[0, :, 256:], mine, sg, su, sd)
    gtok, gwq, gwkv, gwo = back(gnt, resid, cotangent, tokens, normed, q, kv, p, att, wq, wkv, wo, gmisc)
    shared_pieces = scatter(shared_grads, PIECE[3:], ORDERS[3:], cid=2)
    pq, po, pkv = scatter([gwq, gwo, gwkv], PIECE[:3], ORDERS[:3], cid=4)
    pm = pkv[0, :12, 256:].astype(f32)
    return (
        block_out,
        gtok,
        unpack(pq, 12),
        unpack(pkv[:, :, :128], 12),
        unpack(pkv[:, :, 128:256], 12),
        unpack(po, 12),
        unpack(shared_pieces[0], 12),
        unpack(shared_pieces[1], 12),
        unpack(shared_pieces[2], 8),
        pm[:, :64],
        pm[:, 64],
        pm[:, 65],
        gg[None],
        gu[None],
        gd[None],
    )


def solution(mesh):
    in_specs = (
        P(("fsdp", "rep"), None),
        P(("fsdp", "rep"), None),
        P(("fsdp", "rep"), None),
        P(("fsdp", "rep"), None),
        P(("fsdp", "rep"), None),
        P(("fsdp", "rep"), None),
        P(("fsdp", "rep"), None),
        P(("fsdp", "rep"), None),
        P(("fsdp", "rep"), None),
        P(("fsdp", "rep"), None),
        P(("fsdp", "rep"), None),
        P(("fsdp", "rep"), None),
        P(("fsdp", "rep")),
        P(("fsdp", "rep")),
        P("fsdp", None, "rep"),
        P("fsdp", None, "rep"),
        P("fsdp", "rep", None),
    )
    out_specs = (
        P(("fsdp", "rep"), None),
        P(("fsdp", "rep"), None),
        P(("fsdp", "rep"), None),
        P(("fsdp", "rep"), None),
        P(("fsdp", "rep"), None),
        P(("fsdp", "rep"), None),
        P(("fsdp", "rep"), None),
        P(("fsdp", "rep"), None),
        P(("fsdp", "rep"), None),
        P(("fsdp", "rep"), None),
        P(("fsdp", "rep")),
        P(("fsdp", "rep")),
        P("fsdp", None, "rep"),
        P("fsdp", None, "rep"),
        P("fsdp", "rep", None),
    )
    return jax.shard_map(local, mesh=mesh, in_specs=in_specs, out_specs=out_specs, check_vma=False)
```

time: 4670 us -> 522 us (0.11)
  waiting for transfers between devices: 1780 us -> 0 us
  blocking collectives: 1740 us -> 0 us
  starting transfers between devices: 616 us -> 0 us
  Pallas kernels: 0 us -> 480 us
  local copies, waits for them, and re-layouts: 335 us -> 26.5 us
  matrix products: 115 us -> 0 us
    all_gather x10 -> x0, waiting for transfers between devices: 1690 us -> none  [the longest x1 311 us: local(): lax.all_gather(query_weight, ('fsdp', 'rep'), axis=0, tiled=True)]
    unnamed x3 -> x0, blocking collectives: 1370 us -> none
    unnamed x224 -> x0, starting transfers between devices: 580 us -> none
    pallas_call x0 -> x6, Pallas kernels: none -> 480 us  [the longest x1 264 us: moe(): pl.pallas_call(moe_kernel, out_shape=[sds((TOK, D)), sds((TOK, D), f32),...]
    all_gather x1 -> x0, blocking collectives: 364 us -> none  [local(): lax.all_gather(router_weight, ('fsdp', 'rep'), axis=0, tiled=True)]
    unnamed x503 -> x35, local copies, waits for them, and re-layouts: 270 us -> 16.8 us
    dot_general x39 -> x0, matrix products: 115 us -> none  [the longest x8 27 us: left_transposed(): lax.dot_general(left, right, (((0,), (0,)), ((), ())), preferred_element_...]
    all_to_all x4 -> x0, waiting for transfers between devices: 79 us -> none  [the longest x1 43.1 us: local(): lax.all_to_all(grad_outgoing, 'fsdp', split_axis=0, concat_axis=0, tiled=...]
  transfers between devices with their start and end apart: 242 -> 0, of which waited for: 10 -> 0; matrix products, arithmetic and copies ran while one was open for 37% -> 0% of each run, Pallas kernels for 0% -> 0%
where the time goes in v1:
time: 522 us; the launch traced here: 514 us
  Pallas kernels  480 us (92%)
  local copies, waits for them, and re-layouts  26.5 us (5%)
  other arithmetic  5.3 us (1%)
    pallas_call x1, Pallas kernels, moe(): pl.pallas_call(moe_kernel, out_shape=[sds((TOK, D)), sds((TOK, D), f32),...  264 us
    pallas_call x2, Pallas kernels, scatter(): pl.pallas_call(functools.partial(scatter_kernel, n=n, rows=rows, piece=pi...  114 us
    pallas_call x1, Pallas kernels, gather(): pl.pallas_call(functools.partial(gather_kernel, n=n, rows=rows, piece=pie...  69.5 us
    pallas_call x2, Pallas kernels, call(): pl.pallas_call(body, out_shape=outs, in_specs=[pl.BlockSpec(memory_space=...  33.2 us
    unnamed x35, local copies, waits for them, and re-layouts  16.8 us

profile of v1, /device:TPU:1, one launch (start us, length us, event | category | flops | bytes accessed | tf_op | source)
XLA Modules:
  0.0 513.6 jit_solution(9231791340449772370)
XLA Ops:
  0.6 0.7 copy.37
  1.4 0.8 copy.38
  2.1 0.1 pad.33.clone
  2.2 0.8 maximum_maximum_fusion
  3.0 0.7 reshape.113
  3.8 0.7 reshape.114
  4.5 0.8 reshape.111
  5.4 0.8 reshape.112
  6.3 0.8 reshape.115
  7.1 0.8 reshape.116
  7.9 0.7 pad.26.refs_5_
  8.6 69.5 %gather_weights.1 = (bf16[2,2,4,2,4,48,384]{6,5,4,3,2,1,0:T(8,128)(2,1)S(1)}, bf16[2,2,4,2,4,48,384]{6,5,4,3,2,1,0:T(8,128)(2,1)}, bf16[2,2,4,2,4,48,384]{6,5,4,...) custom-call(bf16[4,16,384]{2,1,0:T(8,128)(2,1)S(1)} %pad.21.refs_0_,, ...), custom_call_target="tpu_custom_call" | custom-call | tf_op jit(solution)/shard_map/gather_weights/pallas_call | solution.py:156
  78.1 0.0 copy-start
  78.1 2.2 copy-done
  80.3 0.0 copy-start.1
  80.3 1.7 copy-done.1
  82.0 0.0 copy-start.2
  82.0 1.7 copy-done.2
  83.7 1.6 copy-done.3
  85.4 1.4 copy.43.routes
  86.8 11.7 %attend.1 = (bf16[128,1536]{1,0:T(8,128)(2,1)}, bf16[4,128,384]{2,1,0:T(8,128)(2,1)}, bf16[4,128,256]{2,1,0:T(8,128)(2,1)}, f32[4,384,128]{2,1,0:T(8,128)}, bf16...) custom-call(bf16[128,1536]{1,0:T(8,128)(2,1)} %tokens.3, ...), custom_call_target="tpu_custom_call" | custom-call | tf_op jit(solution)/shard_map/attend/pallas_call | solution.py:489
  98.5 1.8 slice_bitcast_fusion.router_r
  100.3 264.2 %moe.1 = (bf16[128,1536]{1,0:T(8,128)(2,1)}, f32[128,1536]{1,0:T(8,128)}, f32[1536,128]{1,0:T(8,128)}, f32[1536,256]{1,0:T(8,128)}, f32[1536,256]{1,0:T(8,128)},...) custom-call(bf16[128,1536]{1,0:T(8,128)(2,1)} %get-tuple-element.51., ...), custom_call_target="tpu_custom_call" | custom-call | tf_op jit(solution)/shard_map/moe/pallas_call | solution.py:796
  364.5 56.8 %scatter_grads.3 = (bf16[4,16,256]{2,1,0:T(8,128)(2,1)}, bf16[4,16,256]{2,1,0:T(8,128)(2,1)}, bf16[4,16,384]{2,1,0:T(8,128)(2,1)}) custom-call(bf16[2,2,4,2,4,48,256]{6,5,4,3,2,1,0:T(8,128)(2,1)} %bitcast.89, bf16[2,2,4,2,4,48,256]{6,5,4,3,2,1,0:T(8,128)(2,1)} %bitcast.90, bf16[2,2,4,2,4,32,384]{6,5,4,3,2,1,0:T(8,128)(2,1)} %bitcast.91), custom_call_target="tpu_custom_call" | custom-call | tf_op jit(solution)/shard_map/scatter_grads/pallas_call | solution.py:323
  421.3 0.8 convert_bitcast_fusion.2
  422.2 0.6 copy.54
  422.9 0.6 copy.55
  423.5 1.4 slice_convert_fusion
  424.9 21.5 %back.1 = (f32[128,1536]{1,0:T(8,128)}, bf16[4,1536,384]{2,1,0:T(8,128)(2,1)}, bf16[4,1536,384]{2,1,0:T(8,128)(2,1)}, bf16[4,1536,384]{2,1,0:T(8,128)(2,1)}) custom-call(f32[128,1536]{1,0:T(8,128)} %get-tuple-element.58.gnt, f32[128,1536]{1,0:T(8,128)} %get-tuple-element.53.resid_h.resid_r, bf16[128,1536]{1,0:T(8,128)(2,1)} %cot.1, ...), custom_call_target="tpu_custom_call" | custom-call | tf_op jit(solution)/shard_map/back/pallas_call | solution.py:489
  446.4 56.7 %scatter_grads.2 = (bf16[4,16,384]{2,1,0:T(8,128)(2,1)}, bf16[4,16,384]{2,1,0:T(8,128)(2,1)}, bf16[4,16,384]{2,1,0:T(8,128)(2,1)}) custom-call(bf16[2,2,4,2,4,48,384]{6,5,4,3,2,1,0:T(8,128)(2,1)} %bitcast.86, bf16[2,2,4,2,4,48,384]{6,5,4,3,2,1,0:T(8,128)(2,1)} %bitcast.88, bf16[2,2,4,2,4,48,384]{6,5,4,3,2,1,0:T(8,128)(2,1)} %bitcast.87), custom_call_target="tpu_custom_call" | custom-call | tf_op jit(solution)/shard_map/scatter_grads/pallas_call | solution.py:323
  503.1 0.0 copy-start.5
  503.2 1.0 convert_bitcast_fusion
  504.2 0.6 copy.50
  504.9 0.6 copy.53
  505.5 0.7 convert_bitcast_fusion.4
  506.3 0.6 copy.51
  506.9 0.6 copy.52
  507.6 0.7 bitcast_convert_fusion
  508.2 0.7 slice_reduce_fusion
  508.9 0.0 copy-done.7
  508.9 0.7 copy.68
  509.7 0.0 copy-done.6
  509.7 1.1 copy.69
  510.8 0.0 copy-done.5
  510.8 1.1 copy.70
  512.0 0.0 copy-done.8
  512.0 0.0 copy-done.4
  512.0 1.1 copy.71
  (31 shorter events, 0.4 us)
Async XLA Ops:
  78.1 2.2 copy-start
  80.3 1.7 copy-start.1
  82.0 1.7 copy-start.2
  83.7 1.6 copy-start.3
  446.4 62.5 %copy-start.7 = (bf16[128,1536]{1,0:T(8,128)(2,1)S(1)}, bf16[128,1536]{1,0:T(8,128)(2,1)}, u32[]{:S(2)}) copy-start(bf16[128,1536]{1,0:T(8,128)(2,1)} %get-tuple-element.104) | copy-start | bytes 1179652
  446.4 63.3 %copy-start.6 = (f32[1536,256]{1,0:T(8,128)S(1)}, f32[1536,256]{1,0:T(8,128)}, u32[]{:S(2)}) copy-start(f32[1536,256]{1,0:T(8,128)} %get-tuple-element.78) | copy-start | bytes 4718596
  503.1 7.7 %copy-start.5 = (f32[1536,256]{1,0:T(8,128)S(1)}, f32[1536,256]{1,0:T(8,128)}, u32[]{:S(2)}) copy-start(f32[1536,256]{1,0:T(8,128)} %get-tuple-element.79) | copy-start | bytes 4718596
  508.2 3.7 copy-start.8
  509.7 2.3 copy-start.4
